TPU v7x, 32 devices: a whole 2x2x4 slice. The times are simulated.
32 devices in a mesh: leaf: 4 (over x, core), front: 8 (over z, y).
Axes of the slice: x: 2, y: 2, z: 4, core: 2. Of those that a mesh axis runs over, the one named last changes fastest.
Arguments:
- front_matrix: float32 [4, 2048, 2048], P('leaf', 'front'), as said below
- child_blocks: float32 [32, 4, 3, 128, 128], P(('leaf', 'front')), may hold values from -0.046875 to 0.046875
- child_target: int32 [32, 4, 3], P(('leaf', 'front')), may hold values from 0 to 31, as said below
- child_count: int32 [32, 4], P(('leaf', 'front')), may hold values from 1 to 3, as said below
- shot_rhs: float32 [4, 64, 2048], P('leaf'), may hold values from -6 to 6
Outputs:
- factored: float32 [4, 2048, 2048], P('leaf', 'front')
- eliminated: float32 [4, 64, 2048], P('leaf')
Inputs may be any that keep to these rules, and one draw needn't show every extreme that they name: `child_target`: A bucket's code places its block on a row block that the receiving device (leaf index of the bucket, front index of the sender) holds, at a column block no later than that row block. Slots from child_count on are empty and hold no data. In every draw some leaf index receives 3 live blocks from every sender. `front_matrix`: after the child blocks are added, the symmetric matrix that each front's lower triangle defines is positive definite.
All inputs are finite; a program needn't handle non-finite values.
Results may differ from a plain program's by a relative error of at most 0.00013.
Values sent between devices are 32-bit elements; how exact they have to be, the bound alone decides.
A program may use at most 64 MiB of HBM per device.

v0:
```python
import jax
import jax.numpy as jnp
from jax import lax
from jax.sharding import PartitionSpec as P

BLOCK = 128
PIVOTS = 1024


def lower_sym(square):
    return jnp.tril(square) + jnp.swapaxes(jnp.tril(square, -1), -1, -2)


def right_solve(factor, values):
    solved = jax.scipy.linalg.solve_triangular(factor, jnp.swapaxes(values, 1, 2), lower=True)
    return jnp.swapaxes(solved, 1, 2)


def local(front_matrix, child_blocks, child_target, child_count, shot_rhs):
    fronts_here, rows_local, order_here = front_matrix.shape
    leaf_count = lax.axis_size("leaf")
    capacity = child_blocks.shape[2]
    slot_ids = lax.broadcasted_iota(jnp.int32, child_target.shape, 2)
    live_code = jnp.where(slot_ids < child_count[:, :, None], child_target, -1)
    arrived, codes = (
        lax.all_to_all(child_blocks, "leaf", split_axis=1, concat_axis=1, tiled=True),
        lax.all_to_all(live_code, "leaf", split_axis=1, concat_axis=1, tiled=True),
    )
    count_in = leaf_count * capacity
    flat_blocks = arrived.reshape(count_in, BLOCK * BLOCK)
    flat_codes = codes.reshape(count_in)
    block_cols = order_here // BLOCK
    block_rows = rows_local // BLOCK
    slot_total = fronts_here * block_rows * block_cols
    one_hot = (
        lax.broadcasted_iota(jnp.int32, (slot_total, count_in), 0) == flat_codes[None, :]
    ).astype(jnp.float32)
    summed = jnp.dot(
        one_hot, flat_blocks, precision=lax.Precision.HIGHEST, preferred_element_type=jnp.float32
    )
    extended = summed.reshape(fronts_here, block_rows, block_cols, BLOCK, BLOCK)
    extended = extended.transpose(0, 1, 3, 2, 4).reshape(fronts_here, rows_local, order_here)
    matrix = front_matrix + extended
    my_index = lax.axis_index("front")
    row_global = my_index * rows_local + lax.broadcasted_iota(jnp.int32, (rows_local, 1), 0)
    full_rows = lax.broadcasted_iota(jnp.int32, (order_here, 1), 0)
    current_rhs = shot_rhs
    left_parts = []
    diag_parts = []
    solved_parts = []
    for pivot_step in range(PIVOTS // BLOCK):
        start_col = pivot_step * BLOCK
        end_col = start_col + BLOCK
        column_panel = matrix[:, :, start_col:end_col]
        full_column = lax.all_gather(column_panel, "front", axis=1, tiled=True)
        pivot_factor = jnp.linalg.cholesky(lower_sym(full_column[:, start_col:end_col]))
        full_panel = right_solve(pivot_factor, full_column)
        full_panel = jnp.where(full_rows < start_col, jnp.float32(0.0), full_panel)
        full_panel = full_panel.at[:, start_col:end_col].set(pivot_factor)
        my_panel = lax.dynamic_slice_in_dim(full_panel, my_index * rows_local, rows_local, 1)
        tail_panel = full_panel[:, end_col:]
        update = jnp.einsum(
            "frb,fcb->frc",
            my_panel,
            tail_panel,
            precision=lax.Precision.HIGHEST,
            preferred_element_type=jnp.float32,
        )
        matrix = matrix.at[:, :, end_col:].add(-update)
        zeta = right_solve(pivot_factor, current_rhs[:, :, start_col:end_col])
        rhs_update = jnp.einsum(
            "fnb,fcb->fnc",
            zeta,
            tail_panel,
            precision=lax.Precision.HIGHEST,
            preferred_element_type=jnp.float32,
        )
        current_rhs = current_rhs.at[:, :, end_col:].add(-rhs_update)
        pivots_now = jnp.diagonal(pivot_factor, axis1=1, axis2=2)
        left_parts.append(my_panel / pivots_now[:, None, :])
        diag_parts.append(pivots_now * pivots_now)
        solved_parts.append(zeta * pivots_now[:, None, :])
    col_global = lax.broadcasted_iota(jnp.int32, (1, order_here), 1)
    combined = jnp.concatenate(left_parts + [matrix[:, :, PIVOTS:]], axis=2)
    combined = jnp.where(row_global < col_global, jnp.float32(0.0), combined)
    diag_full = jnp.concatenate(
        diag_parts + [jnp.zeros((fronts_here, order_here - PIVOTS), jnp.float32)], axis=1
    )
    on_diagonal = (row_global == col_global) & (col_global < PIVOTS)
    factored = jnp.where(on_diagonal, diag_full[:, None, :], combined)
    eliminated = jnp.concatenate(solved_parts + [current_rhs[:, :, PIVOTS:]], axis=2)
    return (factored, eliminated)


def solution(mesh):
    return jax.shard_map(
        local,
        mesh=mesh,
        in_specs=(
            P("leaf", "front", None),
            P(("leaf", "front"), None, None, None, None),
            P(("leaf", "front"), None, None),
            P(("leaf", "front"), None),
            P("leaf", None, None),
        ),
        out_specs=(P("leaf", "front", None), P("leaf", None, None)),
        check_vma=False,
    )
```

profile of v0, /device:TPU:21, one launch (start us, length us, event | category | flops | bytes accessed | tf_op | source)
XLA Modules:
  0.0 618.2 jit_solution(13146817966217290256)
XLA Ops:
  39.6 37.8 %all-gather.9.cloned.1.call-done = f32[1,2048,128]{1,2,0:T(8,128)} async-done(((f32[1,256,128]{1,2,0:T(8,128)}), f32[1,2048,128]{1,2,0:T(8,128)}) %all-gather.9.cloned.1.call-update) | async-done | bytes 1048592 | tf_op jit(solution)/shard_map/all_gather | solution.py:55
  79.4 11.7 %custom-call.46 = f32[1,128,128]{2,1,0:T(8,128)S(1)} custom-call(f32[1,128,128]{2,1,0:T(8,128)S(1)} %copy.164), custom_call_target="Cholesky" | custom-call | tf_op jit(solution)/shard_map/jit(cholesky)/cholesky | solution.py:56
  92.4 9.8 %custom-call.47 = f32[1,128,128]{1,2,0:T(8,128)S(1)} custom-call(f32[1,128,128]{2,1,0:T(8,128)S(1)} %get-tuple-element.308), custom_call_target="InvertDiagBlocksLowerTriangular" | custom-call | tf_op jit(solution)/shard_map/jit(_solve_triangular)/triangular_solve | solution.py:15
  110.4 38.0 %all-gather.11.cloned.1.call-done = f32[1,2048,128]{1,2,0:T(8,128)} async-done(((f32[1,256,128]{1,2,0:T(8,128)}), f32[1,2048,128]{1,2,0:T(8,128)}) %all-gather.11.cloned.1.call-update) | async-done | bytes 1048592 | tf_op jit(solution)/shard_map/all_gather | solution.py:55
  150.4 11.7 %custom-call.48 = f32[1,128,128]{2,1,0:T(8,128)S(1)} custom-call(f32[1,128,128]{2,1,0:T(8,128)S(1)} %copy.172), custom_call_target="Cholesky" | custom-call | tf_op jit(solution)/shard_map/jit(cholesky)/cholesky | solution.py:56
  163.4 9.8 %custom-call.49 = f32[1,128,128]{1,2,0:T(8,128)S(1)} custom-call(f32[1,128,128]{2,1,0:T(8,128)S(1)} %get-tuple-element.306), custom_call_target="InvertDiagBlocksLowerTriangular" | custom-call | tf_op jit(solution)/shard_map/jit(_solve_triangular)/triangular_solve | solution.py:15
  181.1 38.3 %all-gather.13.cloned.1.call-done = f32[1,2048,128]{1,2,0:T(8,128)} async-done(((f32[1,256,128]{1,2,0:T(8,128)}), f32[1,2048,128]{1,2,0:T(8,128)}) %all-gather.13.cloned.1.call-update) | async-done | bytes 1048592 | tf_op jit(solution)/shard_map/all_gather | solution.py:55
  221.4 11.7 %custom-call.50 = f32[1,128,128]{2,1,0:T(8,128)S(1)} custom-call(f32[1,128,128]{2,1,0:T(8,128)S(1)} %copy.180), custom_call_target="Cholesky" | custom-call | tf_op jit(solution)/shard_map/jit(cholesky)/cholesky | solution.py:56
  234.5 9.8 %custom-call.51 = f32[1,128,128]{1,2,0:T(8,128)S(1)} custom-call(f32[1,128,128]{2,1,0:T(8,128)S(1)} %get-tuple-element.304), custom_call_target="InvertDiagBlocksLowerTriangular" | custom-call | tf_op jit(solution)/shard_map/jit(_solve_triangular)/triangular_solve | solution.py:15
  258.7 32.6 %all-gather.15.cloned.1.call-done = f32[1,2048,128]{1,2,0:T(8,128)} async-done(((f32[1,256,128]{1,2,0:T(8,128)}), f32[1,2048,128]{1,2,0:T(8,128)}) %all-gather.15.cloned.1.call-update) | async-done | bytes 1048592 | tf_op jit(solution)/shard_map/all_gather | solution.py:55
  293.9 12.5 %custom-call.52 = f32[1,128,128]{2,1,0:T(8,128)S(1)} custom-call(f32[1,128,128]{2,1,0:T(8,128)} %fusion.94), custom_call_target="Cholesky" | custom-call | tf_op jit(solution)/shard_map/jit(cholesky)/cholesky | solution.py:56
  308.3 11.3 %custom-call.53 = f32[1,128,128]{1,2,0:T(8,128)} custom-call(f32[1,128,128]{2,1,0:T(8,128)} %get-tuple-element.302), custom_call_target="InvertDiagBlocksLowerTriangular" | custom-call | tf_op jit(solution)/shard_map/jit(_solve_triangular)/triangular_solve | solution.py:15
  337.2 28.3 %all-gather.17.cloned.1.call-done = f32[1,2048,128]{2,1,0:T(8,128)} async-done(((f32[1,256,128]{2,1,0:T(8,128)}), f32[1,2048,128]{2,1,0:T(8,128)}) %all-gather.17.cloned.1.call-update) | async-done | bytes 1048592 | tf_op jit(solution)/shard_map/all_gather | solution.py:55
  367.4 11.7 %custom-call.54 = f32[1,128,128]{2,1,0:T(8,128)S(1)} custom-call(f32[1,128,128]{2,1,0:T(8,128)S(1)} %fusion.90), custom_call_target="Cholesky" | custom-call | tf_op jit(solution)/shard_map/jit(cholesky)/cholesky | solution.py:56
  380.6 9.8 %custom-call.55 = f32[1,128,128]{1,2,0:T(8,128)S(1)} custom-call(f32[1,128,128]{2,1,0:T(8,128)S(1)} %get-tuple-element.300), custom_call_target="InvertDiagBlocksLowerTriangular" | custom-call | tf_op jit(solution)/shard_map/jit(_solve_triangular)/triangular_solve | solution.py:15
  407.0 28.6 %all-gather.19.cloned.1.call-done = f32[1,2048,128]{2,1,0:T(8,128)} async-done(((f32[1,256,128]{2,1,0:T(8,128)}), f32[1,2048,128]{2,1,0:T(8,128)}) %all-gather.19.cloned.1.call-update) | async-done | bytes 1048592 | tf_op jit(solution)/shard_map/all_gather | solution.py:55
  437.7 11.7 %custom-call.56 = f32[1,128,128]{2,1,0:T(8,128)S(1)} custom-call(f32[1,128,128]{2,1,0:T(8,128)S(1)} %fusion.86), custom_call_target="Cholesky" | custom-call | tf_op jit(solution)/shard_map/jit(cholesky)/cholesky | solution.py:56
  450.7 9.8 %custom-call.57 = f32[1,128,128]{1,2,0:T(8,128)S(1)} custom-call(f32[1,128,128]{2,1,0:T(8,128)S(1)} %get-tuple-element.298), custom_call_target="InvertDiagBlocksLowerTriangular" | custom-call | tf_op jit(solution)/shard_map/jit(_solve_triangular)/triangular_solve | solution.py:15
  480.5 26.4 %all-gather.21.cloned.1.call-done = f32[1,2048,128]{2,1,0:T(8,128)} async-done(((f32[1,256,128]{2,1,0:T(8,128)}), f32[1,2048,128]{2,1,0:T(8,128)}) %all-gather.21.cloned.1.call-update) | async-done | bytes 1048592 | tf_op jit(solution)/shard_map/all_gather | solution.py:55
  508.8 11.7 %custom-call.58 = f32[1,128,128]{2,1,0:T(8,128)S(1)} custom-call(f32[1,128,128]{2,1,0:T(8,128)S(1)} %fusion.82), custom_call_target="Cholesky" | custom-call | tf_op jit(solution)/shard_map/jit(cholesky)/cholesky | solution.py:56
  521.9 9.8 %custom-call.59 = f32[1,128,128]{1,2,0:T(8,128)S(1)} custom-call(f32[1,128,128]{2,1,0:T(8,128)S(1)} %get-tuple-element.296), custom_call_target="InvertDiagBlocksLowerTriangular" | custom-call | tf_op jit(solution)/shard_map/jit(_solve_triangular)/triangular_solve | solution.py:15
  545.6 32.2 %all-gather.23.cloned.1.call-done = f32[1,2048,128]{2,1,0:T(8,128)} async-done(((f32[1,256,128]{2,1,0:T(8,128)}), f32[1,2048,128]{2,1,0:T(8,128)}) %all-gather.23.cloned.1.call-update) | async-done | bytes 1048592 | tf_op jit(solution)/shard_map/all_gather | solution.py:55
  579.8 11.7 %custom-call.60 = f32[1,128,128]{2,1,0:T(8,128)S(1)} custom-call(f32[1,128,128]{2,1,0:T(8,128)S(1)} %fusion.78), custom_call_target="Cholesky" | custom-call | tf_op jit(solution)/shard_map/jit(cholesky)/cholesky | solution.py:56
  593.0 9.8 %custom-call.61 = f32[1,128,128]{1,2,0:T(8,128)S(1)} custom-call(f32[1,128,128]{2,1,0:T(8,128)S(1)} %get-tuple-element.294), custom_call_target="InvertDiagBlocksLowerTriangular" | custom-call | tf_op jit(solution)/shard_map/jit(_solve_triangular)/triangular_solve | solution.py:15
  (249 shorter events, 165.9 us)
Async XLA Ops:
  14.9 14.9 %all-to-all-start.1 = ((f32[1,4,3,128,128]{4,3,2,0,1:T(8,128)}), f32[1,4,3,128,128]{4,3,2,0,1:T(8,128)S(1)}, u32[]{:S(2)}, u32[]{:S(2)}) async-start(f32[1,4,3,128,128]{4,3,2,0,1:T(8,128)} %bitcast.515), calls=%async_computation.1 | async-start | bytes 1572864 | tf_op jit(solution)/shard_map/all_to_all | solution.py:26
  19.1 58.3 %all-gather.9.cloned.1.call-start = ((), (), s32[]{:S(2)}) async-start(), calls=%async_computation.2 | async-start | bytes 1179648 | tf_op jit(solution)/shard_map/all_gather | solution.py:55
  38.9 109.5 %all-gather.11.cloned.1.call-start = ((), (), s32[]{:S(2)}) async-start(), calls=%async_computation.3 | async-start | bytes 1179648 | tf_op jit(solution)/shard_map/all_gather | solution.py:55
  102.2 5.6 copy-start.20
  109.8 109.6 %all-gather.13.cloned.1.call-start = ((), (), s32[]{:S(2)}) async-start(), calls=%async_computation.4 | async-start | bytes 1179648 | tf_op jit(solution)/shard_map/all_gather | solution.py:55
  173.2 5.7 copy-start.18
  180.9 110.4 %all-gather.15.cloned.1.call-start = ((), (), s32[]{:S(2)}) async-start(), calls=%async_computation.5 | async-start | bytes 1179648 | tf_op jit(solution)/shard_map/all_gather | solution.py:55
  244.3 6.8 %copy-start.23 = (f32[1,128,128]{1,2,0:T(8,128)}, f32[1,128,128]{1,2,0:T(8,128)S(1)}, u32[]{:S(2)}) copy-start(f32[1,128,128]{1,2,0:T(8,128)S(1)} %custom-call.51) | copy-start | bytes 196612
  252.7 112.7 %all-gather.17.cloned.1.call-start = ((), (), s32[]{:S(2)}) async-start(), calls=%async_computation.6 | async-start | bytes 1179648 | tf_op jit(solution)/shard_map/all_gather | solution.py:55
  319.5 4.9 copy-start.8
  324.4 6.9 %copy-start.21 = (f32[1,128,128]{1,2,0:T(8,128)S(1)}, f32[1,128,128]{1,2,0:T(8,128)}, u32[]{:S(2)}) copy-start(f32[1,128,128]{1,2,0:T(8,128)} %copy-done.20) | copy-start | bytes 196612
  327.7 107.9 %all-gather.19.cloned.1.call-start = ((), (), s32[]{:S(2)}) async-start(), calls=%async_computation.7 | async-start | bytes 1179648 | tf_op jit(solution)/shard_map/all_gather | solution.py:55
  395.9 7.2 %copy-start.24 = (f32[1,128,128]{1,2,0:T(8,128)S(1)}, f32[1,128,128]{1,2,0:T(8,128)}, u32[]{:S(2)}) copy-start(f32[1,128,128]{1,2,0:T(8,128)} %copy-done.23) | copy-start | bytes 196612
  396.6 110.2 %all-gather.21.cloned.1.call-start = ((), (), s32[]{:S(2)}) async-start(), calls=%async_computation.8 | async-start | bytes 1179648 | tf_op jit(solution)/shard_map/all_gather | solution.py:55
  462.7 5.3 copy-start.5
  462.7 6.0 copy-start.22
  467.1 7.2 %copy-start.7 = (f32[1,2048,128]{2,1,0:T(8,128)S(1)}, f32[1,2048,128]{2,1,0:T(8,128)}, u32[]{:S(2)}) copy-start(f32[1,2048,128]{2,1,0:T(8,128)} %copy-done.6) | copy-start | bytes 3145732
  467.1 7.9 %copy-start.26 = (f32[1,128,128]{1,2,0:T(8,128)S(1)}, f32[1,128,128]{1,2,0:T(8,128)}, u32[]{:S(2)}) copy-start(f32[1,128,128]{1,2,0:T(8,128)} %copy-done.25) | copy-start | bytes 196612
  467.8 110.0 %all-gather.23.cloned.1.call-start = ((), (), s32[]{:S(2)}) async-start(), calls=%async_computation.9 | async-start | bytes 1179648 | tf_op jit(solution)/shard_map/all_gather | solution.py:55
  534.0 5.5 copy-start.16
  545.6 61.5 %copy-start.15 = (f32[1,256,2048]{2,1,0:T(8,128)S(1)}, f32[1,256,2048]{2,1,0:T(8,128)}, u32[]{:S(2)}) copy-start(f32[1,256,2048]{2,1,0:T(8,128)} %divide_dynamic-update-slice_fusion.1) | copy-start | bytes 6291460
  545.6 61.5 %copy-start.14 = (f32[1,256,1152]{2,1,0:T(8,128)S(1)}, f32[1,256,1152]{2,1,0:T(8,128)}, u32[]{:S(2)}) copy-start(f32[1,256,1152]{2,1,0:T(8,128)} %copy-done.13) | copy-start | bytes 3538948
  604.0 4.1 copy-start.17
  604.0 4.1 copy-start.27
  (15 other events, 34.1 us)
Sparse Core Ops, SparseCore 0:
  39.0 38.3 all-gather.8
  109.9 38.4 all-gather.10
  181.0 38.4 all-gather.12
  252.8 38.4 all-gather.14
  327.9 37.5 all-gather.16
  396.7 38.8 all-gather.18
  467.9 38.8 all-gather.20
  538.9 38.8 all-gather.22
where the time goes:
time: 628 us; the launch traced here: 618 us
  waiting for transfers between devices  269 us (43%)
  other arithmetic  212 us (34%)
  matrix products  62.4 us (10%)
  local copies, waits for them, and re-layouts  46.6 us (7%)
  between operations  15.7 us (2%)
  starting transfers between devices  6.44 us (1%)
  blocking collectives  6.28 us (1%)
    all_gather x8, waiting for transfers between devices, local(): full_column = lax.all_gather(column_panel, 'front', axis=1, tiled=True)  262 us
    another operation x32, other arithmetic, local(): jnp.linalg.cholesky(lower_sym(full_column[:, start_col:end_col]))  106 us
    another operation x8, other arithmetic, right_solve(): jax.scipy.linalg.solve_triangular(factor, jnp.swapaxes(values, 1, 2), low...  79.9 us
    another operation x16, matrix products, right_solve(): jax.scipy.linalg.solve_triangular(factor, jnp.swapaxes(values, 1, 2), low...  31 us
    dot_general x8, matrix products, local(): jnp.einsum('fnb,fcb->fnc', zeta, tail_panel, precision=lax.Precision.HIGH...  15.3 us
    dot_general x8, matrix products, local(): jnp.einsum('frb,fcb->frc', my_panel, tail_panel, precision=lax.Precision....  14.8 us
  transfers between devices with their start and end apart: 9, of which 9 were waited for; matrix products, arithmetic and copies ran while one was open for 8% of the time, Pallas kernels for 0%

commit v1 on v0

v1 whole, which is shorter than its diff:
```python
import functools

import jax
import jax.numpy as jnp
from jax import lax
from jax.experimental import pallas as pl
from jax.experimental.pallas import tpu as pltpu
from jax.sharding import PartitionSpec as P

BLOCK = 128
PIVOTS = 1024
STEPS = PIVOTS // BLOCK
PANEL = 8
MESH = pl.DeviceIdType.MESH
NT = (((1,), (1,)), ((), ()))
TN = (((0,), (0,)), ((), ()))


def split(value):
    high = value.astype(jnp.bfloat16)
    low = (value - high.astype(jnp.float32)).astype(jnp.bfloat16)
    return high, low


def dot3(left, right):
    dot = functools.partial(lax.dot_general, dimension_numbers=NT, preferred_element_type=jnp.float32)
    return dot(left[0], right[0]) + (dot(left[0], right[1]) + dot(left[1], right[0]))


def panel_factor(panel, start):
    lead = pltpu.roll(panel[:, :BLOCK], lax.rem(BLOCK - start, BLOCK), 1)
    full = (PANEL, BLOCK)
    entry = [[jnp.broadcast_to(lead[i : i + 1, j : j + 1], full) for j in range(i + 1)] for i in range(PANEL)]
    lower = [[None] * PANEL for _ in range(PANEL)]
    for j in range(PANEL):
        inverse = 1.0 / entry[j][j]
        for i in range(j + 1, PANEL):
            lower[i][j] = entry[i][j] * inverse
        for i in range(j + 1, PANEL):
            for k in range(j + 1, i + 1):
                entry[i][k] = entry[i][k] - lower[i][j] * entry[k][j]
    rows = lax.broadcasted_iota(jnp.int32, full, 0)
    inverse = [[None] * PANEL for _ in range(PANEL)]
    left, right = panel[:, :BLOCK], panel[:, BLOCK:]
    new_left, new_right = left, right
    for j in range(PANEL):
        column = jnp.zeros(full, jnp.float32)
        for i in range(j + 1, PANEL):
            total = lower[i][j]
            for k in range(j + 1, i):
                total = total + lower[i][k] * inverse[k][j]
            inverse[i][j] = -total
            column = jnp.where(rows == i, -total, column)
        if j < PANEL - 1:
            new_left = new_left + column * left[j : j + 1]
            new_right = new_right + column * right[j : j + 1]
    pivots = entry[0][0]
    for i in range(1, PANEL):
        pivots = jnp.where(rows == i, entry[i][i], pivots)
    return new_left, new_right, pivots


def block_factor(work):
    def body(index, carry):
        start = pl.multiple_of(index * PANEL, PANEL)
        left, right, pivots = panel_factor(work[pl.ds(start, PANEL), :], start)
        work[pl.ds(start, PANEL), :BLOCK] = left
        work[pl.ds(start, PANEL), BLOCK:] = right
        lanes = lax.broadcasted_iota(jnp.int32, left.shape, 1)
        scaled = jnp.where(lanes >= start + PANEL, left / pivots, 0.0)
        both = jnp.concatenate([left, right], axis=1)
        work[...] -= lax.dot_general(
            scaled, both, TN, precision=lax.Precision.HIGHEST, preferred_element_type=jnp.float32
        )
        return carry

    lax.fori_loop(0, BLOCK // PANEL, body, 0)


def kernel(
    leafs, fronts, front, child, codes, rhs, out, elim,
    child_in, codes_in, mine, top, high, low, lead, work, own_w, far_w, tail_out, tail_in,
    child_send, child_recv, code_send, code_recv, top_send, top_recv, relay_send,
    far_send, far_recv, tail_send, tail_recv,
):
    rows, order = front.shape
    shots = rhs.shape[0]
    slots = child.shape[1]
    col_blocks = order // BLOCK
    row_blocks = rows // BLOCK
    tops = PIVOTS // rows
    slab = fronts // 4
    me = lax.axis_index("front")
    leaf = lax.axis_index("leaf")
    depth = me // slab
    here = me < tops
    below = me >= tops

    def to(front_id):
        return {"front": front_id}

    def remote(src, dst, send, recv, device):
        return pltpu.make_async_remote_copy(
            src_ref=src, dst_ref=dst, send_sem=send, recv_sem=recv, device_id=device, device_id_type=MESH
        )

    barrier = pltpu.get_barrier_semaphore()
    for i in range(1, leafs):
        pl.semaphore_signal(barrier, inc=1, device_id={"leaf": lax.rem(leaf + i, leafs)}, device_id_type=MESH)
    for i in range(1, fronts):
        pl.semaphore_signal(barrier, inc=1, device_id=to(lax.rem(me + i, fronts)), device_id_type=MESH)
    pl.semaphore_wait(barrier, leafs + fronts - 2)

    def child_copies(i):
        peer = lax.rem(leaf + i, leafs)
        device = {"leaf": peer}
        return (
            remote(child.at[peer], child_in.at[i], child_send.at[i], child_recv.at[i], device),
            remote(codes.at[peer], codes_in.at[i], code_send.at[i], code_recv.at[i], device),
        )

    for i in range(1, leafs):
        for copy in child_copies(i):
            copy.start()
    child_in[0] = child[leaf]
    codes_in[0] = codes[leaf]
    for i in range(1, leafs):
        for copy in child_copies(i):
            copy.wait()

    def assemble(column, carry):
        lanes = pl.ds(pl.multiple_of(column * BLOCK, BLOCK), BLOCK)
        for r in range(row_blocks):
            total = front[r * BLOCK : (r + 1) * BLOCK, lanes]
            place = r * col_blocks + column
            for i in range(leafs):
                for j in range(slots):
                    hit = codes_in[i, j : j + 1, :] == place
                    total = total + jnp.where(hit, child_in[i, j], 0.0)
            mine[column, r * BLOCK : (r + 1) * BLOCK, :] = total
        return carry

    lax.fori_loop(0, col_blocks, assemble, 0)

    def owner_rows(owner):
        return pl.ds(owner * rows, rows)

    def last_column(owner):
        return min(STEPS, (owner + 1) * row_blocks)

    def top_copy(owner, column, target):
        place = top.at[column, owner_rows(owner)]
        return remote(mine.at[column], place, top_send.at[column, target], top_recv.at[owner, column], to(target))

    def relay_copy(owner, column):
        place = top.at[column, owner_rows(owner)]
        target = lax.rem(me + slab, fronts)
        return remote(place, place, relay_send.at[owner, column], top_recv.at[owner, column], to(target))

    def owners(column):
        return [o for o in range(tops) if column < last_column(o)]

    for column in range(STEPS):
        for owner in owners(column):

            @pl.when(me == owner)
            def _():
                for target in range(3 * slab):
                    if target != owner:
                        top_copy(owner, column, target).start()
                top[column, owner * rows : (owner + 1) * rows, :] = mine[column]

    def arrive(column):
        for owner in owners(column):

            @pl.when(me != owner)
            def _():
                top_copy(owner, column, 0).wait_recv()

            @pl.when(depth == 2)
            def _():
                relay_copy(owner, column).start()

    def far_copy(column, target):
        return remote(
            own_w.at[column], far_w.at[me - tops, column], far_send.at[column, target],
            far_recv.at[me - tops, column], to(tops + target),
        )

    arrive(0)
    row_id = lax.broadcasted_iota(jnp.int32, (BLOCK, BLOCK), 0)
    col_id = lax.broadcasted_iota(jnp.int32, (BLOCK, BLOCK), 1)
    for step in range(STEPS):
        begin, end = step * BLOCK, (step + 1) * BLOCK
        lanes = slice(begin, end)
        current = jnp.concatenate([top[step, begin:, :], rhs[:, lanes], mine[step]], axis=0)
        if step:
            past = slice(0, begin)
            current = current - dot3(
                (high[begin:, past], low[begin:, past]), (high[begin:end, past], low[begin:end, past])
            )
        square = current[:BLOCK]
        work[:, :BLOCK] = jnp.where(row_id >= col_id, square, 0.0) + jnp.where(row_id > col_id, square, 0.0).T
        work[:, BLOCK:] = jnp.where(row_id == col_id, 1.0, 0.0)
        block_factor(work)
        if step + 1 < STEPS:
            arrive(step + 1)
        upper = work[:, :BLOCK]
        on_diag = jnp.where(row_id == col_id, upper, 0.0)
        pivots = jnp.sum(on_diag, axis=0, keepdims=True)
        pivots_down = jnp.sum(on_diag, axis=1, keepdims=True)
        value = dot3(split(current[BLOCK:]), split(work[:, BLOCK:]))
        weighted = value * lax.rsqrt(pivots)
        high[end:, lanes], low[end:, lanes] = split(weighted)
        unit = value / pivots
        if step:
            lead[begin - BLOCK : begin, :] = jnp.zeros((BLOCK, BLOCK), jnp.float32)
        lead[begin:end, :] = on_diag + jnp.where(col_id > row_id, upper / pivots_down, 0.0).T
        inside = PIVOTS - end
        if inside:
            lead[end:, :] = unit[:inside]
        elim[:, lanes] = value[inside : inside + shots]

        @pl.when(here)
        def _():
            out[:, lanes] = lead[pl.ds(pl.multiple_of(me * rows, rows), rows), :]

        @pl.when(below)
        def _():
            out[:, lanes] = unit[inside + shots :]
            own_w[step] = weighted[inside + shots :]
            for target in range(1, fronts - tops):

                @pl.when(me < tops + target)
                def _():
                    far_copy(step, target).start()

    def tail_copy(source, target_step):
        target = lax.rem(source + target_step, fronts)
        return remote(
            tail_out, tail_in.at[source - tops], tail_send.at[target_step], tail_recv.at[source - tops], to(target)
        )

    first = PIVOTS + shots

    @pl.when(below)
    def _():
        lanes = pl.ds(pl.multiple_of(PIVOTS + (me - tops) * rows, BLOCK), rows)
        shot = (high[PIVOTS:first, :], low[PIVOTS:first, :])
        tail = rhs[:, lanes] - dot3(shot, (high[first:, :], low[first:, :]))
        tail_out[...] = tail
        for i in range(1, fronts):
            tail_copy(me, i).start()
        tail_in[me - tops] = tail

    for part in range(fronts - tops):
        source = tops + part
        lanes = slice(PIVOTS + part * rows, PIVOTS + (part + 1) * rows)
        base = STEPS + part * row_blocks

        def pieces():
            return jnp.concatenate([mine[base + r] for r in range(row_blocks)], axis=1)

        @pl.when(me < source)
        def _():
            out[:, lanes] = jnp.zeros((rows, rows), jnp.float32)

        @pl.when(me == source)
        def _():
            own = (high[first:, :], low[first:, :])
            result = pieces() - dot3(own, own)
            r = lax.broadcasted_iota(jnp.int32, result.shape, 0)
            c = lax.broadcasted_iota(jnp.int32, result.shape, 1)
            out[:, lanes] = jnp.where(r >= c, result, 0.0)

        @pl.when(me > source)
        def _():
            for step in range(STEPS):
                remote(
                    own_w.at[step], far_w.at[part, step], far_send.at[step, 0], far_recv.at[part, step], to(source)
                ).wait_recv()
            other = jnp.concatenate([far_w[part, step] for step in range(STEPS)], axis=1)
            out[:, lanes] = pieces() - dot3((high[first:, :], low[first:, :]), split(other))

    for part in range(fronts - tops):

        @pl.when(me != tops + part)
        def _():
            remote(
                tail_out, tail_in.at[part], tail_send.at[0], tail_recv.at[part], to(tops + part)
            ).wait_recv()

        elim[:, PIVOTS + part * rows : PIVOTS + (part + 1) * rows] = tail_in[part]

    for column in range(STEPS):
        for owner in owners(column):

            @pl.when(me == owner)
            def _():
                for target in range(3 * slab):
                    if target != owner:
                        top_copy(owner, column, target).wait_send()

            @pl.when(depth == 2)
            def _():
                relay_copy(owner, column).wait_send()

        for target in range(1, fronts - tops):

            @pl.when(below & (me < tops + target))
            def _():
                far_copy(column, target).wait_send()

    @pl.when(below)
    def _():
        for i in range(1, fronts):
            tail_copy(me, i).wait_send()


def local(front_matrix, child_blocks, child_target, child_count, shot_rhs):
    _, rows, order = front_matrix.shape
    leafs, fronts = lax.axis_size("leaf"), lax.axis_size("front")
    slots = child_blocks.shape[2]
    shots = shot_rhs.shape[1]
    slot_ids = lax.broadcasted_iota(jnp.int32, child_target.shape, 2)
    live = jnp.where(slot_ids < child_count[:, :, None], child_target, -1)[0]
    codes = jnp.pad(live, ((0, 0), (0, 8 - slots)), constant_values=-1)
    codes = jnp.broadcast_to(codes[:, :, None], (leafs, 8, BLOCK))
    tops = PIVOTS // rows
    parts = fronts - tops
    stack = PIVOTS + shots + rows
    f32 = jnp.float32
    dma = pltpu.SemaphoreType.DMA
    vmem = pl.BlockSpec(memory_space=pltpu.VMEM)
    factored, eliminated = pl.pallas_call(
        functools.partial(kernel, leafs, fronts),
        out_shape=(jax.ShapeDtypeStruct((rows, order), f32), jax.ShapeDtypeStruct((shots, order), f32)),
        in_specs=[vmem] * 4,
        out_specs=(vmem, vmem),
        scratch_shapes=[
            pltpu.VMEM((leafs, slots, BLOCK, BLOCK), f32),
            pltpu.VMEM((leafs, 8, BLOCK), jnp.int32),
            pltpu.VMEM((order // BLOCK, rows, BLOCK), f32),
            pltpu.VMEM((STEPS, PIVOTS, BLOCK), f32),
            pltpu.VMEM((stack, PIVOTS), jnp.bfloat16),
            pltpu.VMEM((stack, PIVOTS), jnp.bfloat16),
            pltpu.VMEM((PIVOTS, BLOCK), f32),
            pltpu.VMEM((BLOCK, 2 * BLOCK), f32),
            pltpu.VMEM((STEPS, rows, BLOCK), f32),
            pltpu.VMEM((parts, STEPS, rows, BLOCK), f32),
            pltpu.VMEM((shots, rows), f32),
            pltpu.VMEM((parts, shots, rows), f32),
            dma((leafs,)),
            dma((leafs,)),
            dma((leafs,)),
            dma((leafs,)),
            dma((STEPS, fronts)),
            dma((tops, STEPS)),
            dma((tops, STEPS)),
            dma((STEPS, parts)),
            dma((parts, STEPS)),
            dma((fronts,)),
            dma((parts,)),
        ],
        compiler_params=pltpu.CompilerParams(
            collective_id=0, has_side_effects=True, vmem_limit_bytes=56 * 1024 * 1024
        ),
        cost_estimate=pl.CostEstimate(
            flops=6 * stack * PIVOTS * PIVOTS, bytes_accessed=8 * rows * order, transcendentals=0
        ),
    )(front_matrix[0], child_blocks[0], codes, shot_rhs[0])
    return factored[None], eliminated[None]


def solution(mesh):
    return jax.shard_map(
        local,
        mesh=mesh,
        in_specs=(
            P("leaf", "front", None),
            P(("leaf", "front"), None, None, None, None),
            P(("leaf", "front"), None, None),
            P(("leaf", "front"), None),
            P("leaf", None, None),
        ),
        out_specs=(P("leaf", "front", None), P("leaf", None, None)),
        check_vma=False,
    )
```

time: 628 us -> 157 us (0.25); the launches traced: 618 us -> 157 us
  waiting for transfers between devices: 269 us -> 0 us
  other arithmetic: 212 us -> 0.69 us
  Pallas kernels: 0 us -> 151 us
  matrix products: 62.4 us -> 0 us
  local copies, waits for them, and re-layouts: 46.6 us -> 4.77 us
  between operations: 15.7 us -> 0.65 us
  starting transfers between devices: 6.44 us -> 0 us
  blocking collectives: 6.28 us -> 0 us
    all_gather x8 -> x0, waiting for transfers between devices: 262 us -> none  [local(): full_column = lax.all_gather(column_panel, 'front', axis=1, tiled=True)]
    another operation x40 -> x0, other arithmetic: 186 us -> none  [the longest x32 106 us: local(): jnp.linalg.cholesky(lower_sym(full_column[:, start_col:end_col]))]
    pallas_call x0 -> x1, Pallas kernels: none -> 151 us  [local(): pl.pallas_call(functools.partial(kernel, leafs, fronts), out_shape=(jax.S...]
    dot_general x17 -> x0, matrix products: 31.5 us -> none  [the longest x8 15.3 us: local(): jnp.einsum('fnb,fcb->fnc', zeta, tail_panel, precision=lax.Precision.HIGH...]
    another operation x16 -> x0, matrix products: 31 us -> none  [right_solve(): jax.scipy.linalg.solve_triangular(factor, jnp.swapaxes(values, 1, 2), low...]
    slice x22 -> x0, local copies, waits for them, and re-layouts: 12.7 us -> none  [the longest x14 6.52 us: local(): full_column[:, start_col:end_col]]
    add x11 -> x0, other arithmetic: 10.3 us -> none  [the longest x9 7.23 us: lower_sym(): return jnp.tril(square) + jnp.swapaxes(jnp.tril(square, -1), -1, -2)]
    gather x8 -> x0, local copies, waits for them, and re-layouts: 10.2 us -> none  [local(): pivots_now = jnp.diagonal(pivot_factor, axis1=1, axis2=2)]
  transfers between devices with their start and end apart: 9 -> 0, of which waited for: 9 -> 0; matrix products, arithmetic and copies ran while one was open for 8% -> 0% of each run, Pallas kernels for 0% -> 0%
where the time goes in v1:
time: 157 us
  Pallas kernels  151 us (96%)
  local copies, waits for them, and re-layouts  4.77 us (3%)
    pallas_call x1, Pallas kernels, local(): pl.pallas_call(functools.partial(kernel, leafs, fronts), out_shape=(jax.S...  151 us
    unnamed x4, local copies, waits for them, and re-layouts  3.99 us

profile of v1, /device:TPU:21, one launch (start us, length us, event | category | flops | bytes accessed | tf_op | source)
XLA Modules:
  0.0 157.2 jit_solution(11941969218899872618)
XLA Ops:
  0.6 0.7 compare_select_fusion
  1.3 0.1 copy.7
  1.4 0.7 broadcast_in_dim.18.codes
  2.1 151.1 %shard_map.71 = (f32[256,2048]{1,0:T(8,128)}, f32[64,2048]{1,0:T(8,128)}) custom-call(f32[256,2048]{1,0:T(8,128)} %bitcast.11, f32[4,3,128,128]{3,2,1,0:T(8,128)} %bitcast.12, s32[4,8,128]{2,1,0:T(8,128)} %broadcast_in_dim.18.codes, f32[64,2048]{1,0:T(8,128)} %bitcast.13), custom_call_target="tpu_custom_call" | custom-call | flops 8455716864 | bytes 4194304 | tf_op jit(solution)/shard_map/pallas_call | solution.py:335
  153.2 0.0 copy-start
  153.2 3.2 %copy.10 = f32[1,256,2048]{2,1,0:T(8,128)} copy(f32[1,256,2048]{2,1,0:T(8,128)} %bitcast.7) | data formatting | bytes 4194304
  156.4 0.0 copy-done
  156.4 0.8 copy.11
  (1 shorter events, 0.0 us)
Async XLA Ops:
  153.2 3.2 %copy-start = (f32[64,2048]{1,0:T(8,128)S(1)}, f32[64,2048]{1,0:T(8,128)}, u32[]{:S(2)}) copy-start(f32[64,2048]{1,0:T(8,128)} %get-tuple-element.5) | copy-start | bytes 1572868

commit v2 on v1

--- a/solution.py
+++ b/solution.py
@@ -27,59 +27,80 @@
     return dot(left[0], right[0]) + (dot(left[0], right[1]) + dot(left[1], right[0]))
 
 
-def panel_factor(panel, start):
-    lead = pltpu.roll(panel[:, :BLOCK], lax.rem(BLOCK - start, BLOCK), 1)
-    full = (PANEL, BLOCK)
-    entry = [[jnp.broadcast_to(lead[i : i + 1, j : j + 1], full) for j in range(i + 1)] for i in range(PANEL)]
+def wide(value):
+    return jnp.broadcast_to(value, (PANEL, BLOCK))
+
+
+def panel_factor(left, right, start):
+    columns = [wide(left[:, start + j : start + j + 1]) for j in range(PANEL)]
+    entry = [[wide(columns[j][i : i + 1]) for j in range(i + 1)] for i in range(PANEL)]
     lower = [[None] * PANEL for _ in range(PANEL)]
+    reciprocal = []
     for j in range(PANEL):
-        inverse = 1.0 / entry[j][j]
+        reciprocal.append(1.0 / entry[j][j])
         for i in range(j + 1, PANEL):
-            lower[i][j] = entry[i][j] * inverse
+            lower[i][j] = entry[i][j] * reciprocal[j]
         for i in range(j + 1, PANEL):
             for k in range(j + 1, i + 1):
                 entry[i][k] = entry[i][k] - lower[i][j] * entry[k][j]
-    rows = lax.broadcasted_iota(jnp.int32, full, 0)
+    rows = lax.broadcasted_iota(jnp.int32, (PANEL, BLOCK), 0)
     inverse = [[None] * PANEL for _ in range(PANEL)]
-    left, right = panel[:, :BLOCK], panel[:, BLOCK:]
     new_left, new_right = left, right
-    for j in range(PANEL):
-        column = jnp.zeros(full, jnp.float32)
+    for j in range(PANEL - 1):
+        column = jnp.zeros((PANEL, BLOCK), jnp.float32)
         for i in range(j + 1, PANEL):
             total = lower[i][j]
             for k in range(j + 1, i):
                 total = total + lower[i][k] * inverse[k][j]
             inverse[i][j] = -total
             column = jnp.where(rows == i, -total, column)
-        if j < PANEL - 1:
-            new_left = new_left + column * left[j : j + 1]
-            new_right = new_right + column * right[j : j + 1]
-    pivots = entry[0][0]
-    for i in range(1, PANEL):
-        pivots = jnp.where(rows == i, entry[i][i], pivots)
-    return new_left, new_right, pivots
+        new_left = new_left + column * left[j : j + 1]
+        new_right = new_right + column * right[j : j + 1]
+    return new_left, new_right, inverse, reciprocal
+
+
+def halves(value, order):
+    high = value.astype(jnp.bfloat16).astype(jnp.float32)
+    parts = (high, value - high)
+    return jnp.concatenate([parts[i] for i in order], axis=0).astype(jnp.bfloat16)
 
 
 def block_factor(work):
-    def body(index, carry):
-        start = pl.multiple_of(index * PANEL, PANEL)
-        left, right, pivots = panel_factor(work[pl.ds(start, PANEL), :], start)
-        work[pl.ds(start, PANEL), :BLOCK] = left
-        work[pl.ds(start, PANEL), BLOCK:] = right
-        lanes = lax.broadcasted_iota(jnp.int32, left.shape, 1)
-        scaled = jnp.where(lanes >= start + PANEL, left / pivots, 0.0)
-        both = jnp.concatenate([left, right], axis=1)
-        work[...] -= lax.dot_general(
-            scaled, both, TN, precision=lax.Precision.HIGHEST, preferred_element_type=jnp.float32
-        )
-        return carry
-
-    lax.fori_loop(0, BLOCK // PANEL, body, 0)
+    count = BLOCK // PANEL
+    left = [work[i * PANEL : (i + 1) * PANEL, :BLOCK] for i in range(count)]
+    right = [work[i * PANEL : (i + 1) * PANEL, BLOCK:] for i in range(count)]
+    rows = lax.broadcasted_iota(jnp.int32, (PANEL, BLOCK), 0)
+    for b in range(count):
+        start = b * PANEL
+        done_left, done_right, inverse, reciprocal = panel_factor(left[b], right[b], start)
+        work[start : start + PANEL, :BLOCK] = done_left
+        work[start : start + PANEL, BLOCK:] = done_right
+        if b + 1 < count:
+            columns = [wide(left[b + 1][:, start + j : start + j + 1]) for j in range(PANEL)]
+            for j in range(PANEL):
+                factor = columns[j]
+                for k in range(j):
+                    factor = factor + inverse[j][k] * columns[k]
+                factor = factor * reciprocal[j]
+                left[b + 1] = left[b + 1] - factor * done_left[j : j + 1]
+                right[b + 1] = right[b + 1] - factor * done_right[j : j + 1]
+        if b + 2 < count:
+            scale = reciprocal[0]
+            for j in range(1, PANEL):
+                scale = jnp.where(rows == j, reciprocal[j], scale)
+            both = jnp.concatenate([done_left, done_right], axis=1)
+            update = lax.dot_general(
+                halves(done_left * scale, (0, 0, 1)), halves(both, (0, 1, 0)), TN,
+                preferred_element_type=jnp.float32,
+            )
+            for i in range(b + 2, count):
+                left[i] = left[i] - update[i * PANEL : (i + 1) * PANEL, :BLOCK]
+                right[i] = right[i] - update[i * PANEL : (i + 1) * PANEL, BLOCK:]
 
 
 def kernel(
     leafs, fronts, front, child, codes, rhs, out, elim,
-    child_in, codes_in, mine, top, high, low, lead, work, own_w, far_w, tail_out, tail_in,
+    child_in, codes_in, mine, top, high, low, lead, work, column_now, own_w, far_w, tail_out, tail_in,
     child_send, child_recv, code_send, code_recv, top_send, top_recv, relay_send,
     far_send, far_recv, tail_send, tail_recv,
 ):
@@ -190,7 +211,7 @@
     arrive(0)
     row_id = lax.broadcasted_iota(jnp.int32, (BLOCK, BLOCK), 0)
     col_id = lax.broadcasted_iota(jnp.int32, (BLOCK, BLOCK), 1)
-    for step in range(STEPS):
+    def before(step):
         begin, end = step * BLOCK, (step + 1) * BLOCK
         lanes = slice(begin, end)
         current = jnp.concatenate([top[step, begin:, :], rhs[:, lanes], mine[step]], axis=0)
@@ -202,17 +223,21 @@
         square = current[:BLOCK]
         work[:, :BLOCK] = jnp.where(row_id >= col_id, square, 0.0) + jnp.where(row_id > col_id, square, 0.0).T
         work[:, BLOCK:] = jnp.where(row_id == col_id, 1.0, 0.0)
-        block_factor(work)
+        column_now[end:, :] = current[BLOCK:]
+
+    def after(step):
+        begin, end = step * BLOCK, (step + 1) * BLOCK
+        lanes = slice(begin, end)
         if step + 1 < STEPS:
             arrive(step + 1)
         upper = work[:, :BLOCK]
         on_diag = jnp.where(row_id == col_id, upper, 0.0)
         pivots = jnp.sum(on_diag, axis=0, keepdims=True)
         pivots_down = jnp.sum(on_diag, axis=1, keepdims=True)
-        value = dot3(split(current[BLOCK:]), split(work[:, BLOCK:]))
+        value = dot3(split(column_now[end:, :]), split(work[:, BLOCK:]))
         weighted = value * lax.rsqrt(pivots)
         high[end:, lanes], low[end:, lanes] = split(weighted)
-        unit = value / pivots
+        unit = value * (1.0 / pivots)
         if step:
             lead[begin - BLOCK : begin, :] = jnp.zeros((BLOCK, BLOCK), jnp.float32)
         lead[begin:end, :] = on_diag + jnp.where(col_id > row_id, upper / pivots_down, 0.0).T
@@ -234,6 +259,16 @@
                 @pl.when(me < tops + target)
                 def _():
                     far_copy(step, target).start()
+
+    def one_step(index, carry):
+        for step in range(STEPS):
+            pl.when(index == step)(functools.partial(before, step))
+        block_factor(work)
+        for step in range(STEPS):
+            pl.when(index == step)(functools.partial(after, step))
+        return carry
+
+    lax.fori_loop(0, STEPS, one_step, 0)
 
     def tail_copy(source, target_step):
         target = lax.rem(source + target_step, fronts)
@@ -346,6 +381,7 @@
             pltpu.VMEM((stack, PIVOTS), jnp.bfloat16),
             pltpu.VMEM((PIVOTS, BLOCK), f32),
             pltpu.VMEM((BLOCK, 2 * BLOCK), f32),
+            pltpu.VMEM((stack, BLOCK), f32),
             pltpu.VMEM((STEPS, rows, BLOCK), f32),
             pltpu.VMEM((parts, STEPS, rows, BLOCK), f32),
             pltpu.VMEM((shots, rows), f32),

time: 157 us -> 149 us (0.949)
  Pallas kernels: 151 us -> 142 us
    pallas_call x1, Pallas kernels: 151 us -> 142 us  [local(): pl.pallas_call(functools.partial(kernel, leafs, fronts), out_shape=(jax.S...]
where the time goes in v2:
time: 149 us; the launch traced here: 148 us
  Pallas kernels  142 us (95%)
  local copies, waits for them, and re-layouts  4.77 us (3%)
    pallas_call x1, Pallas kernels, local(): pl.pallas_call(functools.partial(kernel, leafs, fronts), out_shape=(jax.S...  142 us
    unnamed x4, local copies, waits for them, and re-layouts  3.99 us

profile of v2, /device:TPU:21, one launch (start us, length us, event | category | flops | bytes accessed | tf_op | source)
XLA Modules:
  0.0 148.4 jit_solution(3584652701871613353)
XLA Ops:
  0.6 0.7 compare_select_fusion
  1.3 0.1 copy.7
  1.4 0.7 broadcast_in_dim.18.codes
  2.1 142.3 %shard_map.71 = (f32[256,2048]{1,0:T(8,128)}, f32[64,2048]{1,0:T(8,128)}) custom-call(f32[256,2048]{1,0:T(8,128)} %bitcast.11, f32[4,3,128,128]{3,2,1,0:T(8,128)} %bitcast.12, s32[4,8,128]{2,1,0:T(8,128)} %broadcast_in_dim.18.codes, f32[64,2048]{1,0:T(8,128)} %bitcast.13), custom_call_target="tpu_custom_call" | custom-call | flops 8455716864 | bytes 4194304 | tf_op jit(solution)/shard_map/pallas_call | solution.py:370
  144.4 0.0 copy-start
  144.4 3.2 %copy.10 = f32[1,256,2048]{2,1,0:T(8,128)} copy(f32[1,256,2048]{2,1,0:T(8,128)} %bitcast.7) | data formatting | bytes 4194304
  147.6 0.0 copy-done
  147.6 0.8 copy.11
  (1 shorter events, 0.0 us)
Async XLA Ops:
  144.4 3.2 %copy-start = (f32[64,2048]{1,0:T(8,128)S(1)}, f32[64,2048]{1,0:T(8,128)}, u32[]{:S(2)}) copy-start(f32[64,2048]{1,0:T(8,128)} %get-tuple-element.5) | copy-start | bytes 1572868
